TPU v7x, 256 devices: a whole 4x4x8 slice. The times are simulated.
256 devices in a mesh: seq: 64 (over y, z_lo, x), tensor: 4 (over z_hi, core).
Axes of the slice: x: 4, y: 4, z: 8 (z_hi: 2, z_lo: 4; z = z_hi * 4 + z_lo), core: 2. Of those that a mesh axis runs over, the one named last changes fastest.
Arguments:
- queries: bfloat16 [32768, 3072], P('seq', 'tensor'), may hold values from -180 to 180, as said below
- ref_keys: bfloat16 [1024, 3072], P('seq', 'tensor'), may hold values from -6 to 6
- ref_values: bfloat16 [1024, 3072], P('seq', 'tensor'), may hold values from -6 to 6
- grad_out: bfloat16 [32768, 3072], P('seq', 'tensor'), may hold values from -12 to 12
- key_weight: bfloat16 [3072, 3072], P(None, 'tensor'), may hold values from -0.109375 to 0.109375
- value_weight: bfloat16 [3072, 3072], P(None, 'tensor'), may hold values from -0.109375 to 0.109375
Outputs:
- grad_queries: bfloat16 [32768, 3072], P('seq', 'tensor')
- grad_ref_rows: bfloat16 [1024, 3072], P('seq', 'tensor')
Inputs may be any that keep to these rules, and one draw needn't show every extreme that they name: `queries`: queries of order one, some rows larger.
All inputs are finite; a program needn't handle non-finite values.
Results may differ from a plain program's by a relative error of at most 0.015.
Values may be sent and summed in bfloat16 or wider, within the bound.
No kernel may reach another device: no remote copies, remote signals or barrier semaphores. Data moves between devices by JAX's collectives and lax.ppermute only.
A program may use at most 128 MiB of HBM per device.

v0:
```python
import jax
import jax.numpy as jnp
from jax import lax
from jax.sharding import PartitionSpec as P

HD = 128


def head_terms(queries, keys_all, values_all, grad_out, head):
    scale = 1.0 / HD**0.5
    lo_col = head * HD
    query_h = queries[:, lo_col : lo_col + HD]
    key_h = keys_all[:, lo_col : lo_col + HD]
    value_h = values_all[:, lo_col : lo_col + HD]
    grad_h = grad_out[:, lo_col : lo_col + HD]
    scores = jnp.dot(query_h, key_h.T, preferred_element_type=jnp.float32) * scale
    probs = jax.nn.softmax(scores, axis=-1)
    probs_b = probs.astype(jnp.bfloat16)
    grad_probs = jnp.dot(grad_h, value_h.T, preferred_element_type=jnp.float32)
    delta = jnp.sum(probs * grad_probs, axis=-1, keepdims=True)
    grad_scores = (probs * (grad_probs - delta)).astype(jnp.bfloat16)
    grad_query = (jnp.dot(grad_scores, key_h, preferred_element_type=jnp.float32) * scale).astype(
        jnp.bfloat16
    )
    grad_key = jnp.dot(grad_scores.T, query_h, preferred_element_type=jnp.float32) * scale
    grad_value = jnp.dot(probs_b.T, grad_h, preferred_element_type=jnp.float32)
    return (grad_query, grad_key, grad_value)


def head_range(queries, keys_all, values_all, grad_out, first, count):
    query_list, key_list, value_list = ([], [], [])
    for head in range(first, first + count):
        grad_query, grad_key, grad_value = head_terms(queries, keys_all, values_all, grad_out, head)
        query_list.append(grad_query)
        key_list.append(grad_key)
        value_list.append(grad_value)
    return (query_list, jnp.concatenate(key_list, axis=1), jnp.concatenate(value_list, axis=1))


def project_exact(keys_own, values_own, key_weight, value_weight):
    key_cols = key_weight.astype(jnp.float32)
    value_cols = value_weight.astype(jnp.float32)
    rows = jnp.dot(
        keys_own, key_cols.T, precision=lax.Precision.HIGHEST, preferred_element_type=jnp.float32
    )
    return rows + jnp.dot(
        values_own,
        value_cols.T,
        precision=lax.Precision.HIGHEST,
        preferred_element_type=jnp.float32,
    )


def shards(queries, ref_keys, ref_values, grad_out, key_weight, value_weight):
    keys_all, values_all = (
        lax.all_gather(ref_keys, "seq", axis=0, tiled=True),
        lax.all_gather(ref_values, "seq", axis=0, tiled=True),
    )
    local_heads = queries.shape[1] // HD
    ranges = (0, local_heads)
    query_list = []
    first, count = ranges
    group_queries, key_terms, value_terms = head_range(
        queries, keys_all, values_all, grad_out, first, count
    )
    query_list = query_list + group_queries
    key_part = key_terms.astype(jnp.bfloat16)
    value_part = value_terms.astype(jnp.bfloat16)
    key_held, value_held = lax.optimization_barrier((key_part, value_part))
    key_wide = key_held.astype(jnp.float32)
    value_wide = value_held.astype(jnp.float32)
    keys_own = lax.psum_scatter(key_wide, "seq", scatter_dimension=0, tiled=True)
    values_own = lax.psum_scatter(value_wide, "seq", scatter_dimension=0, tiled=True)
    partial_value = project_exact(keys_own, values_own, key_weight, value_weight)
    grad_queries = jnp.concatenate(query_list, axis=1)
    grad_rows = lax.psum_scatter(
        partial_value.astype(jnp.bfloat16), "tensor", scatter_dimension=1, tiled=True
    )
    return (grad_queries, grad_rows)


def solution(mesh):
    placed = (
        P("seq", "tensor"),
        P("seq", "tensor"),
        P("seq", "tensor"),
        P("seq", "tensor"),
        P(None, "tensor"),
        P(None, "tensor"),
    )
    return jax.shard_map(
        shards,
        mesh=mesh,
        in_specs=placed,
        out_specs=(P("seq", "tensor"), P("seq", "tensor")),
        check_vma=False,
    )
```

profile of v0, /device:TPU:1, one launch (start us, length us, event | category | flops | bytes accessed | tf_op | source)
XLA Modules:
  0.0 1526.0 jit_solution(15675450137437767035)
XLA Ops:
  7.2 0.7 all-gather.3.cloned.1.call-update
  7.9 0.7 all-gather.5.cloned.1.call-update
  8.7 308.8 %all-gather.3.cloned.1.call-done = bf16[1024,768]{1,0:T(8,128)(2,1)} async-done(((bf16[16,768]{1,0:T(8,128)(2,1)}), bf16[1024,768]{1,0:T(8,128)(2,1)}) %all-gather.3.cloned.1.call-update) | async-done | bytes 1572880 | tf_op jit(solution)/shard_map/all_gather | solution.py:56
  317.5 1.5 multiply_reduce_fusion.11
  319.0 0.5 fusion.2
  319.5 2.3 fusion.25
  321.8 344.2 %all-gather.5.cloned.1.call-done = bf16[1024,768]{1,0:T(8,128)(2,1)} async-done(((bf16[16,768]{1,0:T(8,128)(2,1)}), bf16[1024,768]{1,0:T(8,128)(2,1)}) %all-gather.5.cloned.1.call-update) | async-done | bytes 1572880 | tf_op jit(solution)/shard_map/all_gather | solution.py:57
  666.0 1.7 multiply_reduce_fusion.5
  667.7 0.6 multiply_convert_fusion.5
  669.4 0.5 multiply_reduce_fusion.10
  669.9 0.5 fusion.4
  671.0 0.7 fusion.26
  671.7 0.5 multiply_reduce_fusion.9
  672.2 0.5 fusion.6
  672.7 0.7 fusion.27
  673.4 0.5 multiply_reduce_fusion.8
  673.9 0.5 fusion.8
  674.4 0.7 fusion.28
  675.1 0.5 multiply_reduce_fusion.7
  675.6 0.5 fusion.10
  676.2 0.7 fusion.29
  676.9 0.5 multiply_reduce_fusion.6
  677.4 0.5 fusion.12
  677.9 0.7 fusion.30
  678.6 0.7 copy-done.15
  679.3 0.7 multiply_reduce_fusion.4
  680.5 0.6 multiply_convert_fusion.4
  681.1 0.5 fusion.16
  681.6 0.7 multiply_reduce_fusion.3
  682.3 0.6 multiply_convert_fusion.3
  683.3 0.7 multiply_reduce_fusion.2
  684.0 0.6 multiply_convert_fusion.2
  685.0 0.7 multiply_reduce_fusion.1
  685.8 0.6 multiply_convert_fusion.1
  686.7 0.7 multiply_reduce_fusion
  687.5 0.6 multiply_convert_fusion
  688.1 1.1 copy-done.5
  689.5 2.1 copy.10
  691.7 1.3 copy-done.13
  693.0 2.1 copy.12
  695.4 1.1 copy-done.1
  697.0 1.9 fusion.34
  700.3 361.1 %reduce-scatter.10.cloned.1.call-done = f32[16,768]{1,0:T(8,128)} async-done(((f32[1024,768]{1,0:T(8,128)}), f32[16,768]{1,0:T(8,128)}) %reduce-scatter.10.cloned.1.call-update) | async-done | bytes 49168
  1061.5 6.8 fusion.109
  1068.3 366.2 %reduce-scatter.12.cloned.1.call-done = f32[16,768]{1,0:T(8,128)} async-done(((f32[1024,768]{1,0:T(8,128)}), f32[16,768]{1,0:T(8,128)}) %reduce-scatter.12.cloned.1.call-update) | async-done | bytes 49168
  1434.5 6.7 fusion
  1441.8 1.2 copy.9
  1442.9 76.6 %reduce-scatter.8.cloned.1.call-done = bf16[16,768]{1,0:T(8,128)(2,1)} async-done(((bf16[16,3072]{1,0:T(8,128)(2,1)}), bf16[16,768]{1,0:T(8,128)(2,1)}) %reduce-scatter.8.cloned.1.call-update) | async-done | bytes 24592 | tf_op jit(solution)/shard_map/reduce_scatter | solution.py:76
  (48 shorter events, 6.3 us)
Async XLA Ops:
  7.2 310.3 %all-gather.3.cloned.1.call-start = ((), (), s32[]{:S(2)}) async-start(), calls=%async_computation.3 | async-start | bytes 1597440 | tf_op jit(solution)/shard_map/all_gather | solution.py:56
  7.9 658.1 %all-gather.5.cloned.1.call-start = ((), (), s32[]{:S(2)}) async-start(), calls=%async_computation.4 | async-start | bytes 1597440 | tf_op jit(solution)/shard_map/all_gather | solution.py:57
  8.6 1052.8 %reduce-scatter.10.cloned.1.call-start = ((), (), s32[]{:S(2)}) async-start(), calls=%async_computation.6 | async-start | bytes 3194880
  667.7 1.1 copy-start.14
  667.7 1.7 copy-start
  669.4 1.4 copy-start.11
  669.4 1.6 copy-start.16
  677.9 1.4 copy-start.15
  679.3 1.1 copy-start.12
  681.1 1.3 copy-start.2
  683.0 1.1 copy-start.3
  684.7 1.1 copy-start.7
  686.4 1.1 copy-start.9
  688.1 1.1 copy-start.5
  691.6 1.4 copy-start.13
  691.6 742.9 %reduce-scatter.12.cloned.1.call-start = ((), (), s32[]{:S(2)}) async-start(), calls=%async_computation.7 | async-start | bytes 3194880
  695.1 1.4 copy-start.1
  695.1 824.4 %reduce-scatter.8.cloned.1.call-start = ((), (), s32[]{:S(2)}) async-start(), calls=%async_computation.5 | async-start | bytes 122880 | tf_op jit(solution)/shard_map/reduce_scatter | solution.py:76
  696.5 2.4 copy-start.4
  696.5 2.9 copy-start.8
  697.0 2.9 copy-start.10
  1068.3 373.0 %copy-start.6 = (bf16[512,1024]{1,0:T(8,128)(2,1)S(1)}, bf16[512,1024]{1,0:T(8,128)(2,1)}, u32[]{:S(2)}) copy-start(bf16[512,1024]{1,0:T(8,128)(2,1)} %copy-done.5) | copy-start | bytes 3145732
Sparse Core Ops, SparseCore 0:
  9.8 307.6 all-gather.2
  319.3 346.6 all-gather.4
  691.7 369.6 reduce-scatter.9
  1064.0 370.4 reduce-scatter.11
  1441.4 78.0 reduce-scatter.7
where the time goes:
time: 1530 us
  waiting for transfers between devices  1460 us (95%)
  matrix products  35.2 us (2%)
    unnamed x7, waiting for transfers between devices  729 us
    all_gather x1, waiting for transfers between devices, shards(): lax.all_gather(ref_values, 'seq', axis=0, tiled=True)  344 us
    all_gather x1, waiting for transfers between devices, shards(): lax.all_gather(ref_keys, 'seq', axis=0, tiled=True)  309 us
    reduce_scatter x1, waiting for transfers between devices, shards(): lax.psum_scatter(partial_value.astype(jnp.bfloat16), 'tensor', scatter_di...  76.6 us
  transfers between devices with their start and end apart: 5, of which 5 were waited for; matrix products, arithmetic and copies ran while one was open for 1% of the time, Pallas kernels for 0%

commit v1 on v0

--- a/solution.py
+++ b/solution.py
@@ -53,7 +53,9 @@
 
 def shards(queries, ref_keys, ref_values, grad_out, key_weight, value_weight):
     keys_all, values_all = (
-        lax.all_gather(ref_keys, "seq", axis=0, tiled=True),
+        jnp.concatenate(
+            lax.all_to_all(jnp.stack([ref_keys] * lax.axis_size("seq")), "seq", 0, 0), axis=0
+        ),
         lax.all_gather(ref_values, "seq", axis=0, tiled=True),
     )
     local_heads = queries.shape[1] // HD

time: 1530 us -> 1200 us (0.78)
  waiting for transfers between devices: 1460 us -> 1100 us
    all_gather x1 -> x0, waiting for transfers between devices: 309 us -> none  [shards(): lax.all_gather(ref_keys, 'seq', axis=0, tiled=True)]
    all_gather x1, waiting for transfers between devices: 344 us -> 257 us  [shards(): lax.all_gather(ref_values, 'seq', axis=0, tiled=True)]
    all_to_all x0 -> x1, waiting for transfers between devices: none -> 38.2 us  [shards(): lax.all_to_all(jnp.stack([ref_keys] * lax.axis_size('seq')), 'seq', 0, 0)]
    unnamed x7 -> x6, waiting for transfers between devices: 729 us -> 726 us
  transfers between devices with their start and end apart: 5 -> 5, of which waited for: 5 -> 5; matrix products, arithmetic and copies ran while one was open for 1% -> 3% of each run, Pallas kernels for 0% -> 0%
where the time goes in v1:
time: 1200 us
  waiting for transfers between devices  1100 us (92%)
  matrix products  48.4 us (4%)
  local copies, waits for them, and re-layouts  17.7 us (1%)
  between operations  14 us (1%)
  starting transfers between devices  12.9 us (1%)
    unnamed x6, waiting for transfers between devices  726 us
    all_gather x1, waiting for transfers between devices, shards(): lax.all_gather(ref_values, 'seq', axis=0, tiled=True)  257 us
    reduce_scatter x1, waiting for transfers between devices, shards(): lax.psum_scatter(partial_value.astype(jnp.bfloat16), 'tensor', scatter_di...  74.5 us
    all_to_all x1, waiting for transfers between devices, shards(): lax.all_to_all(jnp.stack([ref_keys] * lax.axis_size('seq')), 'seq', 0, 0)  38.2 us
  transfers between devices with their start and end apart: 5, of which 5 were waited for; matrix products, arithmetic and copies ran while one was open for 3% of the time, Pallas kernels for 0%

profile of v1, /device:TPU:1, one launch (start us, length us, event | category | flops | bytes accessed | tf_op | source)
XLA Modules:
  0.0 1195.8 jit_solution(5844839014325143556)
XLA Ops:
  7.2 2.1 stack.2
  9.2 12.6 %all-to-all-start = ((bf16[64,16,768]{2,1,0:T(8,128)(2,1)}), bf16[64,16,768]{2,1,0:T(8,128)(2,1)S(1)}, u32[]{:S(2)}, u32[]{:S(2)}) async-start(bf16[64,16,768]{2,1,0:T(8,128)(2,1)} %stack.2), calls=%async_computation | async-start | bytes 3145728 | tf_op jit(solution)/shard_map/all_to_all | solution.py:57
  21.8 0.7 all-gather.2.cloned.1.call-update
  22.6 38.2 %all-to-all-done = bf16[64,16,768]{2,1,0:T(8,128)(2,1)S(1)} async-done(((bf16[64,16,768]{2,1,0:T(8,128)(2,1)}), bf16[64,16,768]{2,1,0:T(8,128)(2,1)S(1)}, u32[]{:S(2)}, u32[]{:S(2)}) %all-to-all-start) | async-done | bytes 1572896 | tf_op jit(solution)/shard_map/all_to_all | solution.py:57
  61.8 1.8 multiply_reduce_fusion.10
  63.6 1.8 multiply_reduce_fusion.9
  65.4 1.7 multiply_reduce_fusion.8
  67.1 1.8 multiply_reduce_fusion.7
  68.9 1.5 multiply_reduce_fusion.6
  70.3 2.3 fusion.25
  72.6 256.9 %all-gather.2.cloned.1.call-done = bf16[1024,768]{1,0:T(8,128)(2,1)} async-done(((bf16[16,768]{1,0:T(8,128)(2,1)}), bf16[1024,768]{1,0:T(8,128)(2,1)}) %all-gather.2.cloned.1.call-update) | async-done | bytes 1572880 | tf_op jit(solution)/shard_map/all_gather | solution.py:59
  329.5 2.6 multiply_reduce_fusion.5
  333.2 1.1 fusion.14
  335.8 0.9 copy-done.2
  337.2 0.7 fusion.27
  337.9 0.9 copy-done.1
  339.3 0.7 fusion.28
  340.0 0.9 copy-done
  341.5 0.7 fusion.29
  343.3 0.7 copy-done.22
  344.1 0.7 multiply_reduce_fusion.4
  345.2 0.8 multiply_convert_fusion.4
  346.0 1.1 fusion.16
  347.1 0.7 multiply_reduce_fusion.3
  348.4 1.1 fusion.18
  349.5 0.7 multiply_reduce_fusion.2
  350.9 1.1 fusion.20
  351.9 0.7 multiply_reduce_fusion.1
  353.3 1.1 fusion.22
  354.4 0.7 multiply_reduce_fusion
  355.7 1.0 copy-done.11
  356.7 1.1 fusion.24
  357.8 3.1 copy.10
  361.0 1.3 copy-done.19
  362.3 2.1 copy.12
  364.7 1.1 copy-done.7
  365.8 1.1 fusion.32
  366.9 2.4 fusion.34
  369.4 1.1 fusion.36
  370.5 1.1 fusion.38
  371.6 1.1 fusion.40
  372.8 357.7 %reduce-scatter.10.cloned.1.call-done = f32[16,768]{1,0:T(8,128)} async-done(((f32[1024,768]{1,0:T(8,128)}), f32[16,768]{1,0:T(8,128)}) %reduce-scatter.10.cloned.1.call-update) | async-done | bytes 49168
  730.5 6.1 fusion.109
  736.6 368.0 %reduce-scatter.12.cloned.1.call-done = f32[16,768]{1,0:T(8,128)} async-done(((f32[1024,768]{1,0:T(8,128)}), f32[16,768]{1,0:T(8,128)}) %reduce-scatter.12.cloned.1.call-update) | async-done | bytes 49168
  1104.6 6.8 fusion
  1111.4 1.1 fusion.42
  1112.5 2.3 copy.9
  1114.8 74.5 %reduce-scatter.8.cloned.1.call-done = bf16[16,768]{1,0:T(8,128)(2,1)} async-done(((bf16[16,3072]{1,0:T(8,128)(2,1)}), bf16[16,768]{1,0:T(8,128)(2,1)}) %reduce-scatter.8.cloned.1.call-update) | async-done | bytes 24592 | tf_op jit(solution)/shard_map/reduce_scatter | solution.py:78
  (62 shorter events, 9.7 us)
Async XLA Ops:
  7.2 53.6 %copy-start.20 = (bf16[512,768]{1,0:T(8,128)(2,1)S(1)}, bf16[512,768]{1,0:T(8,128)(2,1)}, u32[]{:S(2)}) copy-start(bf16[512,768]{1,0:T(8,128)(2,1)} %param.6) | copy-start | bytes 2359300
  9.2 51.5 %all-to-all-start = ((bf16[64,16,768]{2,1,0:T(8,128)(2,1)}), bf16[64,16,768]{2,1,0:T(8,128)(2,1)S(1)}, u32[]{:S(2)}, u32[]{:S(2)}) async-start(bf16[64,16,768]{2,1,0:T(8,128)(2,1)} %stack.2), calls=%async_computation | async-start | bytes 3145728 | tf_op jit(solution)/shard_map/all_to_all | solution.py:57
  21.8 307.7 %all-gather.2.cloned.1.call-start = ((), (), s32[]{:S(2)}) async-start(), calls=%async_computation.4 | async-start | bytes 1597440 | tf_op jit(solution)/shard_map/all_gather | solution.py:59
  22.5 708.0 %reduce-scatter.10.cloned.1.call-start = ((), (), s32[]{:S(2)}) async-start(), calls=%async_computation.6 | async-start | bytes 3194880
  60.7 6.4 copy-start.6
  61.3 9.1 copy-start.4
  329.5 2.6 copy-start.5
  332.1 1.1 copy-start.21
  332.1 2.2 copy-start.3
  333.2 1.7 copy-start.17
  333.2 1.9 copy-start.23
  335.1 1.6 copy-start.2
  337.2 1.6 copy-start.1
  339.3 1.6 copy-start
  342.7 1.4 copy-start.22
  344.1 1.1 copy-start.18
  346.0 1.8 copy-start.8
  348.4 1.8 copy-start.9
  350.8 1.8 copy-start.13
  353.3 1.8 copy-start.15
  355.7 1.0 copy-start.11
  360.9 1.4 copy-start.19
  360.9 743.7 %reduce-scatter.12.cloned.1.call-start = ((), (), s32[]{:S(2)}) async-start(), calls=%async_computation.7 | async-start | bytes 3194880
  364.4 1.4 copy-start.7
  364.4 824.9 %reduce-scatter.8.cloned.1.call-start = ((), (), s32[]{:S(2)}) async-start(), calls=%async_computation.5 | async-start | bytes 122880 | tf_op jit(solution)/shard_map/reduce_scatter | solution.py:78
  365.8 3.6 copy-start.10
  365.8 4.7 copy-start.14
  366.9 4.7 copy-start.16
  736.6 374.8 %copy-start.12 = (bf16[512,1024]{1,0:T(8,128)(2,1)S(1)}, bf16[512,1024]{1,0:T(8,128)(2,1)}, u32[]{:S(2)}) copy-start(bf16[512,1024]{1,0:T(8,128)(2,1)} %copy-done.11) | copy-start | bytes 3145732
Sparse Core Ops, SparseCore 0:
  24.4 305.0 all-gather.1
  361.0 369.4 reduce-scatter.9
  733.2 371.3 reduce-scatter.11
  1111.5 77.7 reduce-scatter.7
